TPU v7x, 32 devices: a whole 2x2x4 slice. The times are simulated.
32 devices in a mesh: row: 4 (over y, x), col: 8 (over z, core).
Axes of the slice: x: 2, y: 2, z: 4, core: 2. Of those that a mesh axis runs over, the one named last changes fastest.
Arguments:
- orbitals: bfloat16 [16384, 1024], P('row', 'col'), may hold values from -0.1875 to 0.1875
- kernel: bfloat16 [16384, 16384], P('col', 'row'), may hold values from -6 to 6
- applied: bfloat16 [16384, 256], P('col', 'row'), may hold values from -1.5 to 1.5
- fit: bfloat16 [16384, 16384], P('row', 'col'), may hold values from -0.046875 to 0.046875
Outputs:
- exchange_term: bfloat16 [256, 16384], P('row', 'col')
All inputs are finite; a program needn't handle non-finite values.
Results may differ from a plain program's by a relative error of at most 0.0058.
Values may be sent and summed in bfloat16 or wider, within the bound.
A program may use at most 128 MiB of HBM per device.

v0:
```python
import jax
import jax.numpy as jnp
from jax import lax
from jax.sharding import PartitionSpec as P


def per_device(orbitals, kernel, applied, fit):
    columns = lax.all_gather(orbitals, "row", axis=0, tiled=True)
    nearby = lax.all_to_all(columns, "col", split_axis=0, concat_axis=1, tiled=True)
    density = lax.dot_general(
        nearby,
        lax.all_gather(orbitals, "col", axis=1, tiled=True),
        (((1,), (1,)), ((), ())),
        preferred_element_type=jnp.float32,
    )
    weighted = (density * kernel.astype(jnp.float32)).astype(jnp.bfloat16)
    partial_sum = lax.dot_general(
        weighted,
        lax.all_gather(applied, "row", axis=1, tiled=True),
        (((0,), (0,)), ((), ())),
        preferred_element_type=jnp.float32,
    )
    projected = lax.psum(partial_sum, "col")
    projected_low = projected.astype(jnp.bfloat16)
    result = lax.psum_scatter(
        -lax.dot_general(
            projected_low, fit, (((0,), (0,)), ((), ())), preferred_element_type=jnp.float32
        ),
        "row",
        scatter_dimension=0,
        tiled=True,
    )
    return result.astype(jnp.bfloat16)


def solution(mesh):
    return jax.shard_map(
        per_device,
        mesh=mesh,
        in_specs=(P("row", "col"), P("col", "row"), P("col", "row"), P("row", "col")),
        out_specs=P("row", "col"),
        check_vma=False,
    )
```

profile of v0, /device:TPU:0, one launch (start us, length us, event | category | flops | bytes accessed | tf_op | source)
XLA Modules:
  0.0 413.8 jit_solution(10803505030048609954)
XLA Ops:
  6.5 0.0 all-gather.4.cloned.1.call-start
  6.5 0.7 all-gather.4.cloned.1.call-update
  7.3 0.0 all-gather.6.cloned.1.call-start
  7.3 0.7 all-gather.6.cloned.1.call-update
  8.0 56.6 %all-gather.4.cloned.1.call-done = bf16[16384,128]{1,0:T(8,128)(2,1)} async-done(((bf16[4096,128]{1,0:T(8,128)(2,1)}), bf16[16384,128]{1,0:T(8,128)(2,1)}) %all-gather.4.cloned.1.call-update) | async-done | bytes 4194320 | tf_op jit(solution)/shard_map/all_gather | solution.py:8
  64.6 4.6 %all-to-all-start = ((bf16[8,2048,128]{2,1,0:T(8,128)(2,1)}), bf16[8,2048,128]{2,1,0:T(8,128)(2,1)}, u32[]{:S(2)}, u32[]{:S(2)}) async-start(bf16[8,2048,128]{2,1,0:T(8,128)(2,1)} %bitcast.9), calls=%async_computation | async-start | bytes 8388608 | tf_op jit(solution)/shard_map/all_to_all | solution.py:9
  69.2 0.0 all-gather.8.cloned.1.call-start
  69.3 0.7 all-gather.8.cloned.1.call-update
  70.0 0.0 reduce-scatter.2.cloned.1.call-start
  70.0 160.7 %all-to-all-done = bf16[8,2048,128]{2,1,0:T(8,128)(2,1)} async-done(((bf16[8,2048,128]{2,1,0:T(8,128)(2,1)}), bf16[8,2048,128]{2,1,0:T(8,128)(2,1)}, u32[]{:S(2)}, u32[]{:S(2)}) %all-to-all-start) | async-done | bytes 4194336 | tf_op jit(solution)/shard_map/all_to_all | solution.py:9
  230.8 6.5 %copy.5 = bf16[2048,8,128]{0,2,1:T(8,128)(2,1)} copy(bf16[2048,8,128]{2,0,1:T(8,128)(2,1)} %bitcast.1) | data formatting | bytes 8388608 | tf_op jit(solution)/shard_map/all_to_all | solution.py:9
  237.3 0.0 all-gather.6.cloned.1.call-done
  237.3 25.2 %multiply_convert_fusion = bf16[2048,4096]{1,0:T(8,128)(2,1)} fusion(bf16[2048,4096]{1,0:T(8,128)(2,1)} %param.5, bf16[2048,1024]{0,1:T(8,128)(2,1)} %bitcast.10, bf16[4096,1024]{1,0:T(8,128)(2,1)} %all-gather.6.cloned.1.call-done), kind=kOutput, calls=%fused_computation | convolution fusion | flops 17205035008 | bytes 46137344 | tf_op jit(solution)/shard_map/dot_general | solution.py:10
  262.5 0.0 all-gather.8.cloned.1.call-done
  262.5 12.8 %fusion.1 = f32[4096,256]{1,0:T(8,128)} fusion(bf16[2048,4096]{1,0:T(8,128)(2,1)} %multiply_convert_fusion, bf16[2048,256]{0,1:T(8,128)(2,1)} %all-gather.8.cloned.1.call-done), kind=kOutput, calls=%fused_computation.3 | convolution fusion | flops 4294967296 | bytes 22020096 | tf_op jit(solution)/shard_map/dot_general | solution.py:17
  275.4 86.6 %all-reduce.1 = bf16[4096,256]{1,0:T(8,128)(2,1)S(1)} all-reduce(f32[4096,256]{1,0:T(8,128)} %fusion.1), channel_id=1, replica_groups=mesh['row'=4,'col'=8] {'col'}, use_global_device_ids=true, to_apply=%region_0.0 | all-reduce | flops 1048576 | bytes 6291456 | tf_op jit(solution)/shard_map/psum | solution.py:23
  362.0 9.7 %convolution_negate_fusion = f32[256,2048]{1,0:T(8,128)} fusion(bf16[4096,2048]{1,0:T(8,128)(2,1)} %param.7, bf16[4096,256]{1,0:T(8,128)(2,1)S(1)} %all-reduce.1), kind=kOutput, calls=%fused_computation.1 | convolution fusion | flops 4295491584 | bytes 20971520 | tf_op jit(solution)/shard_map/dot_general | solution.py:26
  371.7 0.0 reduce-scatter.2.cloned.1.call-update
  371.8 33.7 %reduce-scatter.2.cloned.1.call-done = f32[64,2048]{1,0:T(8,128)} async-done(((f32[256,2048]{1,0:T(8,128)}), f32[64,2048]{1,0:T(8,128)}) %reduce-scatter.2.cloned.1.call-update) | async-done | bytes 524304 | tf_op jit(solution)/shard_map/reduce_scatter | solution.py:25
  405.5 1.8 convert_element_type.15
Async XLA Ops:
  6.5 58.1 %all-gather.4.cloned.1.call-start = ((), (), s32[]{:S(2)}) async-start(), calls=%async_computation.2 | async-start | bytes 5242880 | tf_op jit(solution)/shard_map/all_gather | solution.py:8
  7.3 230.1 %all-gather.6.cloned.1.call-start = ((), (), s32[]{:S(2)}) async-start(), calls=%async_computation.3 | async-start | bytes 9437184 | tf_op jit(solution)/shard_map/all_gather | solution.py:12
  64.6 166.1 %all-to-all-start = ((bf16[8,2048,128]{2,1,0:T(8,128)(2,1)}), bf16[8,2048,128]{2,1,0:T(8,128)(2,1)}, u32[]{:S(2)}, u32[]{:S(2)}) async-start(bf16[8,2048,128]{2,1,0:T(8,128)(2,1)} %bitcast.9), calls=%async_computation | async-start | bytes 8388608 | tf_op jit(solution)/shard_map/all_to_all | solution.py:9
  69.2 193.3 %all-gather.8.cloned.1.call-start = ((), (), s32[]{:S(2)}) async-start(), calls=%async_computation.4 | async-start | bytes 1310720 | tf_op jit(solution)/shard_map/all_gather | solution.py:19
  70.0 335.5 %reduce-scatter.2.cloned.1.call-start = ((), (), s32[]{:S(2)}) async-start(), calls=%async_computation.5 | async-start | bytes 2621440 | tf_op jit(solution)/shard_map/reduce_scatter | solution.py:25
Sparse Core Ops, SparseCore 0:
  9.2 55.3 all-gather.3
  66.2 159.5 all-gather.5
  227.7 24.3 all-gather.7
  371.9 33.5 reduce-scatter.1
where the time goes:
time: 414 us
  waiting for transfers between devices  253 us (61%)
  blocking collectives  86.6 us (21%)
  matrix products  47.8 us (12%)
  between operations  13.1 us (3%)
  local copies, waits for them, and re-layouts  6.54 us (2%)
  starting transfers between devices  4.72 us (1%)
    all_to_all x1, waiting for transfers between devices, per_device(): lax.all_to_all(columns, 'col', split_axis=0, concat_axis=1, tiled=True)  161 us
    psum x1, blocking collectives, per_device(): projected = lax.psum(partial_sum, 'col')  86.6 us
    all_gather x1, waiting for transfers between devices, per_device(): columns = lax.all_gather(orbitals, 'row', axis=0, tiled=True)  56.6 us
    reduce_scatter x1, waiting for transfers between devices, per_device(): lax.psum_scatter(-lax.dot_general(projected_low, fit, (((0,), (0,)), ((),...  33.7 us
    dot_general x1, matrix products, per_device(): lax.dot_general(nearby, lax.all_gather(orbitals, 'col', axis=1, tiled=Tru...  25.2 us
    dot_general x1, matrix products, per_device(): lax.dot_general(weighted, lax.all_gather(applied, 'row', axis=1, tiled=Tr...  12.8 us
    dot_general x1, matrix products, per_device(): lax.dot_general(projected_low, fit, (((0,), (0,)), ((), ())), preferred_e...  9.71 us
  transfers between devices with their start and end apart: 5, of which 3 were waited for; matrix products, arithmetic and copies ran while one was open for 8% of the time, Pallas kernels for 0%

commit v1 on v0

--- a/solution.py
+++ b/solution.py
@@ -1,10 +1,268 @@
+import functools
+
 import jax
 import jax.numpy as jnp
 from jax import lax
+from jax.experimental import pallas as pl
+from jax.experimental.pallas import tpu as pltpu
 from jax.sharding import PartitionSpec as P
 
-
-def per_device(orbitals, kernel, applied, fit):
+MESH = pl.DeviceIdType.MESH
+H = 8
+
+
+def gather_kernel(R, C, orb, at, kern, pt, obuf, cbuf, abuf, kbuf,
+                  loc_s, kern_s, up_s, dn_s, sib_s, pl_s, line_r, sib_r, pl_r, a_s, a_r):
+    Z = C // 2
+    N, B = orb.shape
+    NU, M = kern.shape
+    J = at.shape[0]
+    RS = N // H
+    HH = H // 2
+    r = lax.axis_index("row")
+    c = lax.axis_index("col")
+    z = c // 2
+    k = c % 2
+    sib = c + 1 - 2 * k
+    xn = r + 1 - 2 * (r % 2)
+    yn = (r + 2) % 4
+    diag = r == z
+    dx = (r % 2) != (z % 2)
+    dy = (r // 2) != (z // 2)
+
+    kcopy = pltpu.make_async_copy(kern, kbuf, kern_s)
+    kcopy.start()
+
+    def lanes(kk):
+        return pl.ds(pl.multiple_of(kk * B, B), B)
+
+    own = pltpu.make_async_copy(orb, obuf.at[z, :, lanes(k)], loc_s)
+    own.start()
+
+    barrier = pltpu.get_barrier_semaphore()
+    for o in range(R):
+        for kk in range(2):
+            if o == 0 and kk == 1:
+                continue
+            dst = sib if o == 0 else 2 * z + kk
+            pl.semaphore_signal(barrier, inc=1, device_id=((r + o) % R, dst), device_id_type=MESH)
+
+    @pl.when(z > 0)
+    def _():
+        pl.semaphore_signal(barrier, inc=1, device_id=(r, c - 2), device_id_type=MESH)
+
+    @pl.when(z < Z - 1)
+    def _():
+        pl.semaphore_signal(barrier, inc=1, device_id=(r, c + 2), device_id_type=MESH)
+
+    pl.semaphore_wait(barrier, 2 * R - 1 + jnp.where(z > 0, 1, 0) + jnp.where(z < Z - 1, 1, 0))
+    own.wait()
+
+    def rows(q):
+        return pl.ds(pl.multiple_of((q % 2) * (N // 2) + (q // 2) * RS, RS), RS)
+
+    def crows(f):
+        return pl.ds(pl.multiple_of(f * RS, RS), RS)
+
+    def line(zp, q, up):
+        ref = obuf.at[zp, rows(q), lanes(k)]
+        return pltpu.make_async_remote_copy(
+            ref, ref, (up_s if up else dn_s).at[zp, q], line_r.at[zp, q],
+            device_id=(r, c + 2 if up else c - 2), device_id_type=MESH)
+
+    def sibling(zp, q, kk):
+        ref = obuf.at[zp, rows(q), lanes(kk)]
+        return pltpu.make_async_remote_copy(
+            ref, ref, sib_s.at[zp, q], sib_r.at[zp, q], device_id=(r, sib), device_id_type=MESH)
+
+    def from_diag(zp, q):
+        path = (q // 2) % 2
+        return pltpu.make_async_remote_copy(
+            obuf.at[zp, rows(q), lanes(k)], cbuf.at[zp, crows(q // 2), lanes(k)],
+            pl_s.at[zp, q], pl_r.at[zp, k, q // 2],
+            device_id=(jnp.where(path == 0, xn, yn), 2 * z + q % 2), device_id_type=MESH)
+
+    def relay(zp, kk, f):
+        path = f % 2
+        ref = cbuf.at[zp, crows(f), lanes(kk)]
+        last = (path == 0) == dx
+        to = jnp.where(path == 0, jnp.where(dy, xn, yn), jnp.where(dx, yn, xn))
+        return pltpu.make_async_remote_copy(
+            ref, ref, pl_s.at[zp, 2 * f + kk], pl_r.at[zp, kk, f],
+            device_id=(to, c), device_id_type=MESH)
+
+    def relays(f):
+        path = f % 2
+        return jnp.where(path == 0, dx, dy)
+
+    def acopy(o):
+        return pltpu.make_async_remote_copy(
+            at, abuf.at[pl.ds(pl.multiple_of(r * J, J), J)], a_s.at[o], a_r.at[o],
+            device_id=((r + o) % R, c), device_id_type=MESH)
+
+    def do_relay(zp, f):
+        @pl.when(jnp.logical_not(diag))
+        def _():
+            for kk in range(2):
+                desc = relay(zp, kk, f)
+                desc.wait_recv()
+
+                @pl.when(relays(f))
+                def _():
+                    desc.start()
+
+    def spread(zp, q, up, down):
+        if up:
+            @pl.when(z < Z - 1)
+            def _():
+                line(zp, q, True).start()
+        if down:
+            @pl.when(z > 0)
+            def _():
+                line(zp, q, False).start()
+        sibling(zp, q, k).start()
+
+        @pl.when(diag)
+        def _():
+            from_diag(zp, q).start()
+
+    @pl.loop(0, H)
+    def _(q):
+        spread(z, q, True, True)
+
+    for o in range(1, R):
+        acopy(o).start()
+    acp = pltpu.make_async_copy(at, abuf.at[pl.ds(pl.multiple_of(r * J, J), J)], a_s.at[0])
+    acp.start()
+
+    @pl.loop(0, HH)
+    def _(f):
+        do_relay(z, f)
+
+    for d in range(1, Z):
+        below = z - d >= 0
+        above = z + d < Z
+
+        @pl.loop(0, H)
+        def _(q):
+            @pl.when(below)
+            def _():
+                line(z - d, q, True).wait_recv()
+                spread(z - d, q, True, False)
+
+            @pl.when(above)
+            def _():
+                line(z + d, q, False).wait_recv()
+                spread(z + d, q, False, True)
+
+            @pl.when((q % 2 == 1) & (q > 1))
+            def _():
+                @pl.when(below)
+                def _():
+                    do_relay(z - d, q // 2 - 1)
+
+                @pl.when(above)
+                def _():
+                    do_relay(z + d, q // 2 - 1)
+
+        @pl.when(below)
+        def _():
+            do_relay(z - d, HH - 1)
+
+        @pl.when(above)
+        def _():
+            do_relay(z + d, HH - 1)
+
+    @pl.loop(0, Z)
+    def _(zp):
+        @pl.loop(0, H)
+        def _(q):
+            sibling(zp, q, 1 - k).wait_recv()
+
+    half = pl.ds(pl.multiple_of(k * (N // 2), N // 2), N // 2)
+
+    @pl.when(diag)
+    def _():
+        cp = pltpu.make_async_copy(obuf.at[:, half], cbuf, loc_s)
+        cp.start()
+        cp.wait()
+
+    acp.wait()
+    for o in range(1, R):
+        acopy(o).wait_recv()
+    kcopy.wait()
+
+    T = 512
+    S = 512
+
+    @pl.loop(0, M // T)
+    def _(t):
+        mu = pl.ds(pl.multiple_of(t * T, T), T)
+        total = jnp.zeros((abuf.shape[0], T), jnp.float32)
+        for n in range(NU // S):
+            nu = pl.ds(n * S, S)
+            dens = jnp.zeros((S, T), jnp.float32)
+            for zp in range(Z):
+                dens += lax.dot_general(cbuf[zp, nu], obuf[zp, mu], (((1,), (1,)), ((), ())),
+                                        preferred_element_type=jnp.float32)
+            w = (dens * kbuf[nu, mu].astype(jnp.float32)).astype(jnp.bfloat16)
+            total += jnp.dot(abuf[:, nu], w, preferred_element_type=jnp.float32)
+        pt[:, mu] = total
+
+    for o in range(1, R):
+        acopy(o).wait_send()
+
+    @pl.loop(0, Z)
+    def _(zp):
+        @pl.loop(0, H)
+        def _(q):
+            @pl.when((zp <= z) & (z < Z - 1))
+            def _():
+                line(zp, q, True).wait_send()
+
+            @pl.when((zp >= z) & (z > 0))
+            def _():
+                line(zp, q, False).wait_send()
+
+            sibling(zp, q, k).wait_send()
+
+            @pl.when(diag)
+            def _():
+                from_diag(zp, q).wait_send()
+
+            @pl.when(jnp.logical_not(diag) & relays(q // 2))
+            def _():
+                relay(zp, q % 2, q // 2).wait_send()
+
+
+def projected_part(R, C, orbitals, kernel, applied):
+    Z = C // 2
+    N, B = orbitals.shape
+    NU, M = kernel.shape
+    at = applied.T
+    J = at.shape[0]
+    dma = pltpu.SemaphoreType.DMA
+    return pl.pallas_call(
+        functools.partial(gather_kernel, R, C),
+        out_shape=jax.ShapeDtypeStruct((R * J, M), jnp.float32),
+        in_specs=[pl.BlockSpec(memory_space=pl.ANY)] * 3,
+        out_specs=pl.BlockSpec(memory_space=pltpu.VMEM),
+        scratch_shapes=[
+            pltpu.VMEM((Z, N, 2 * B), jnp.bfloat16),
+            pltpu.VMEM((Z, NU, 2 * B), jnp.bfloat16),
+            pltpu.VMEM((R * J, NU), jnp.bfloat16),
+            pltpu.VMEM((NU, M), jnp.bfloat16),
+            dma, dma,
+            dma((Z, H)), dma((Z, H)), dma((Z, H)), dma((Z, H)),
+            dma((Z, H)), dma((Z, H)), dma((Z, 2, H // 2)),
+            dma((R,)), dma((R,)),
+        ],
+        compiler_params=pltpu.CompilerParams(
+            collective_id=0, has_side_effects=True, vmem_limit_bytes=60 * 1024 * 1024),
+    )(orbitals, at, kernel)
+
+
+def plain(orbitals, kernel, applied, fit):
     columns = lax.all_gather(orbitals, "row", axis=0, tiled=True)
     nearby = lax.all_to_all(columns, "col", split_axis=0, concat_axis=1, tiled=True)
     density = lax.dot_general(
@@ -33,7 +291,26 @@
     return result.astype(jnp.bfloat16)
 
 
+def relayed(R, C, orbitals, kernel, applied, fit):
+    partial_sum = projected_part(R, C, orbitals, kernel, applied)
+    projected = lax.psum(partial_sum, "col")
+    result = lax.psum_scatter(
+        -jnp.dot(projected.astype(jnp.bfloat16), fit, preferred_element_type=jnp.float32),
+        "row",
+        scatter_dimension=0,
+        tiled=True,
+    )
+    return result.astype(jnp.bfloat16)
+
+
 def solution(mesh):
+    R, C = mesh.shape["row"], mesh.shape["col"]
+
+    def per_device(orbitals, kernel, applied, fit):
+        if R == 4 and C == 2 * R and orbitals.shape[1] % 128 == 0:
+            return relayed(R, C, orbitals, kernel, applied, fit)
+        return plain(orbitals, kernel, applied, fit)
+
     return jax.shard_map(
         per_device,
         mesh=mesh,

time: 414 us -> 360 us (0.87)
  waiting for transfers between devices: 253 us -> 43.4 us
  Pallas kernels: 0 us -> 182 us
  matrix products: 47.8 us -> 9.65 us
  blocking collectives: 86.6 us -> 109 us
  local copies, waits for them, and re-layouts: 6.54 us -> 0 us
  starting transfers between devices: 4.72 us -> 0.01 us
    pallas_call x0 -> x1, Pallas kernels: none -> 182 us  [projected_part(): pl.pallas_call(functools.partial(gather_kernel, R, C), out_shape=jax.Shap...]
    all_to_all x1 -> x0, waiting for transfers between devices: 161 us -> none  [per_device(): lax.all_to_all(columns, 'col', split_axis=0, concat_axis=1, tiled=True)]
    all_gather x3 -> x0, waiting for transfers between devices: 56.6 us -> none  [the longest x1 56.6 us: per_device(): columns = lax.all_gather(orbitals, 'row', axis=0, tiled=True)]
    dot_general x3 -> x1, matrix products: 47.8 us -> 9.65 us  [relayed(): jnp.dot(projected.astype(jnp.bfloat16), fit, preferred_element_type=jnp.f...]
    psum x1, blocking collectives: 86.6 us -> 109 us  [relayed(): projected = lax.psum(partial_sum, 'col')]
    reduce_scatter x1, waiting for transfers between devices: 33.7 us -> 43.3 us  [relayed(): lax.psum_scatter(-jnp.dot(projected.astype(jnp.bfloat16), fit, preferred_...]
    all_to_all x1 -> x0, local copies, waits for them, and re-layouts: 6.54 us -> none  [per_device(): lax.all_to_all(columns, 'col', split_axis=0, concat_axis=1, tiled=True)]
    all_to_all x1 -> x0, starting transfers between devices: 4.61 us -> none  [per_device(): lax.all_to_all(columns, 'col', split_axis=0, concat_axis=1, tiled=True)]
  transfers between devices with their start and end apart: 5 -> 1, of which waited for: 3 -> 1; matrix products, arithmetic and copies ran while one was open for 8% -> 0% of each run, Pallas kernels for 0% -> 0%
where the time goes in v1:
time: 360 us; the launch traced here: 359 us
  Pallas kernels  182 us (51%)
  blocking collectives  109 us (30%)
  waiting for transfers between devices  43.4 us (12%)
  between operations  13.4 us (4%)
  matrix products  9.65 us (3%)
    pallas_call x1, Pallas kernels, projected_part(): pl.pallas_call(functools.partial(gather_kernel, R, C), out_shape=jax.Shap...  182 us
    psum x1, blocking collectives, relayed(): projected = lax.psum(partial_sum, 'col')  109 us
    reduce_scatter x1, waiting for transfers between devices, relayed(): lax.psum_scatter(-jnp.dot(projected.astype(jnp.bfloat16), fit, preferred_...  43.3 us
    dot_general x1, matrix products, relayed(): jnp.dot(projected.astype(jnp.bfloat16), fit, preferred_element_type=jnp.f...  9.65 us
  transfers between devices with their start and end apart: 1, of which 1 were waited for; matrix products, arithmetic and copies ran while one was open for 0% of the time, Pallas kernels for 0%

profile of v1, /device:TPU:0, one launch (start us, length us, event | category | flops | bytes accessed | tf_op | source)
XLA Modules:
  0.0 359.3 jit_solution(8286400535338626544)
XLA Ops:
  6.5 0.0 reduce-scatter.2.cloned.1.call-start
  6.5 182.5 %shard_map.46 = f32[256,4096]{1,0:T(8,128)} custom-call(bf16[4096,128]{1,0:T(8,128)(2,1)} %orb.1, bf16[64,2048]{1,0:T(8,128)(2,1)} %bitcast.3, bf16[2048,4096]{1,0:T(8,128)(2,1)} %kern.1), custom_call_target="tpu_custom_call" | custom-call | tf_op jit(solution)/shard_map/pallas_call | solution.py:245
  189.0 108.6 %all-reduce.1 = bf16[256,4096]{1,0:T(8,128)(2,1)S(1)} all-reduce(f32[256,4096]{1,0:T(8,128)} %shard_map.46), channel_id=1, replica_groups=mesh['row'=4,'col'=8] {'col'}, use_global_device_ids=true, to_apply=%region_0.0 | all-reduce | flops 1048576 | bytes 6291456 | tf_op jit(solution)/shard_map/psum | solution.py:296
  297.7 9.7 %convolution_negate_fusion = f32[256,2048]{1,0:T(8,128)} fusion(bf16[4096,2048]{1,0:T(8,128)(2,1)} %param.7, bf16[256,4096]{1,0:T(8,128)(2,1)S(1)} %all-reduce.1), kind=kOutput, calls=%fused_computation | convolution fusion | flops 4295491584 | bytes 20971520 | tf_op jit(solution)/shard_map/dot_general | solution.py:298
  307.3 0.0 reduce-scatter.2.cloned.1.call-update
  307.4 43.3 %reduce-scatter.2.cloned.1.call-done = f32[64,2048]{1,0:T(8,128)} async-done(((f32[256,2048]{1,0:T(8,128)}), f32[64,2048]{1,0:T(8,128)}) %reduce-scatter.2.cloned.1.call-update) | async-done | bytes 524304 | tf_op jit(solution)/shard_map/reduce_scatter | solution.py:297
  350.7 1.8 convert_element_type.7
Async XLA Ops:
  6.5 344.2 %reduce-scatter.2.cloned.1.call-start = ((), (), s32[]{:S(2)}) async-start(), calls=%async_computation.1 | async-start | bytes 2621440 | tf_op jit(solution)/shard_map/reduce_scatter | solution.py:297
Sparse Core Ops, SparseCore 0:
  307.5 43.1 reduce-scatter.1

commit v2 on v1

--- a/solution.py
+++ b/solution.py
@@ -9,10 +9,15 @@
 
 MESH = pl.DeviceIdType.MESH
 H = 8
-
-
-def gather_kernel(R, C, orb, at, kern, pt, obuf, cbuf, abuf, kbuf,
-                  loc_s, kern_s, up_s, dn_s, sib_s, pl_s, line_r, sib_r, pl_r, a_s, a_r):
+T = 512
+S = 512
+KS = 4
+
+
+def whole_kernel(R, C, orb, at, kern, fit, out, obuf, cbuf, abuf, kbuf, fbuf,
+                 pown, sout, sin, upin, upout, dnin, dnout, tot, acc, rout, rin,
+                 loc_s, kern_s, fit_s, up_s, dn_s, sib_s, pl_s, line_r, sib_r, pl_r, a_s, a_r,
+                 pair_s, pair_r, pre_s, pre_r, suf_s, suf_r, tot_s, tot_r, red_s, red_r):
     Z = C // 2
     N, B = orb.shape
     NU, M = kern.shape
@@ -30,8 +35,26 @@
     dx = (r % 2) != (z % 2)
     dy = (r // 2) != (z // 2)
 
-    kcopy = pltpu.make_async_copy(kern, kbuf, kern_s)
-    kcopy.start()
+    NT = M // T
+    W = T // 2
+
+    def ktile(t):
+        return pltpu.make_async_copy(
+            kern.at[:, pl.ds(pl.multiple_of(t * T, T), T)], kbuf.at[t % KS], kern_s.at[t % KS])
+
+    for t in range(min(KS, NT)):
+        ktile(t).start()
+    fcopy = pltpu.make_async_copy(fit, fbuf, fit_s)
+    fcopy.start()
+
+    @pl.when(z == 0)
+    def _():
+        upin[...] = jnp.zeros_like(upin)
+
+    @pl.when(z == Z - 1)
+    def _():
+        dnin[...] = jnp.zeros_like(dnin)
+    acc[...] = jnp.zeros_like(acc)
 
     def lanes(kk):
         return pl.ds(pl.multiple_of(kk * B, B), B)
@@ -190,13 +213,26 @@
     acp.wait()
     for o in range(1, R):
         acopy(o).wait_recv()
-    kcopy.wait()
-
-    T = 512
-    S = 512
-
-    @pl.loop(0, M // T)
-    def _(t):
+
+    def pair(t):
+        return pltpu.make_async_remote_copy(
+            sout.at[t], sin.at[t], pair_s.at[t], pair_r.at[t], device_id=(r, sib), device_id_type=MESH)
+
+    def prefix(t):
+        return pltpu.make_async_remote_copy(
+            upout.at[t], upin.at[t], pre_s.at[t], pre_r.at[t], device_id=(r, c + 2), device_id_type=MESH)
+
+    def suffix(t):
+        return pltpu.make_async_remote_copy(
+            dnout.at[t], dnin.at[t], suf_s.at[t], suf_r.at[t], device_id=(r, c - 2), device_id_type=MESH)
+
+    def share(t, kk):
+        ref = tot.at[t, :, pl.ds(pl.multiple_of(kk * W, W), W)]
+        return pltpu.make_async_remote_copy(
+            ref, ref, tot_s.at[t], tot_r.at[t], device_id=(r, sib), device_id_type=MESH)
+
+    def project(t):
+        ktile(t).wait()
         mu = pl.ds(pl.multiple_of(t * T, T), T)
         total = jnp.zeros((abuf.shape[0], T), jnp.float32)
         for n in range(NU // S):
@@ -205,12 +241,112 @@
             for zp in range(Z):
                 dens += lax.dot_general(cbuf[zp, nu], obuf[zp, mu], (((1,), (1,)), ((), ())),
                                         preferred_element_type=jnp.float32)
-            w = (dens * kbuf[nu, mu].astype(jnp.float32)).astype(jnp.bfloat16)
+            w = (dens * kbuf[t % KS, nu].astype(jnp.float32)).astype(jnp.bfloat16)
             total += jnp.dot(abuf[:, nu], w, preferred_element_type=jnp.float32)
-        pt[:, mu] = total
+        first, second = total[:, :W], total[:, W:]
+        pown[t] = jnp.where(k == 0, first, second)
+        sout[t] = jnp.where(k == 0, second, first).astype(jnp.bfloat16)
+        pair(t).start()
+
+        @pl.when(t + KS < NT)
+        def _():
+            ktile(t + KS).start()
+
+    far = jnp.maximum(z, Z - 1 - z)
+
+    @pl.loop(0, NT + Z + 1)
+    def _(s):
+        @pl.when(s < NT)
+        def _():
+            project(s)
+
+        t_pair = s - 1
+
+        @pl.when((t_pair >= 0) & (t_pair < NT))
+        def _():
+            pair(t_pair).wait_recv()
+            pown[t_pair] += sin[t_pair].astype(jnp.float32)
+
+        t_up = s - 1 - z
+
+        @pl.when((t_up >= 0) & (t_up < NT))
+        def _():
+            @pl.when(z > 0)
+            def _():
+                prefix(t_up).wait_recv()
+
+            @pl.when(z < Z - 1)
+            def _():
+                upout[t_up] = (pown[t_up] + upin[t_up].astype(jnp.float32)).astype(jnp.bfloat16)
+                prefix(t_up).start()
+
+        t_dn = s - 1 - (Z - 1 - z)
+
+        @pl.when((t_dn >= 0) & (t_dn < NT))
+        def _():
+            @pl.when(z < Z - 1)
+            def _():
+                suffix(t_dn).wait_recv()
+
+            @pl.when(z > 0)
+            def _():
+                dnout[t_dn] = (pown[t_dn] + dnin[t_dn].astype(jnp.float32)).astype(jnp.bfloat16)
+                suffix(t_dn).start()
+
+        t_tot = s - 1 - far
+
+        @pl.when((t_tot >= 0) & (t_tot < NT))
+        def _():
+            tot[t_tot, :, pl.ds(pl.multiple_of(k * W, W), W)] = (
+                pown[t_tot] + upin[t_tot].astype(jnp.float32) + dnin[t_tot].astype(jnp.float32)
+            ).astype(jnp.bfloat16)
+            share(t_tot, k).start()
+
+        t_ex = s - 2 - far
+
+        @pl.when((t_ex >= 0) & (t_ex < NT))
+        def _():
+            share(t_ex, 1 - k).wait_recv()
+
+            @pl.when(t_ex == 0)
+            def _():
+                fcopy.wait()
+            acc[...] += jnp.dot(
+                tot[t_ex], fbuf[pl.ds(pl.multiple_of(t_ex * T, T), T)], preferred_element_type=jnp.float32)
+
+    def quarter(o):
+        return pltpu.make_async_remote_copy(
+            rout.at[o - 1], rin.at[o - 1], red_s.at[o - 1], red_r.at[o - 1],
+            device_id=((r + o) % R, c), device_id_type=MESH)
+
+    def rows_of(rr):
+        return pl.ds(pl.multiple_of(rr * J, J), J)
+
+    for o in (2, 1, 3)[: R - 1]:
+        rout[o - 1] = acc[rows_of((r + o) % R)].astype(jnp.bfloat16)
+        quarter(o).start()
+    result = acc[rows_of(r)]
+    for o in range(1, R):
+        quarter(o).wait_recv()
+        result += rin[o - 1].astype(jnp.float32)
+    out[...] = (-result).astype(jnp.bfloat16)
 
     for o in range(1, R):
         acopy(o).wait_send()
+        quarter(o).wait_send()
+
+    @pl.loop(0, NT)
+    def _(t):
+        pair(t).wait_send()
+        share(t, k).wait_send()
+
+        @pl.when(z < Z - 1)
+        def _():
+            prefix(t).wait_send()
+
+        @pl.when(z > 0)
+        def _():
+            suffix(t).wait_send()
 
     @pl.loop(0, Z)
     def _(zp):
@@ -235,31 +371,43 @@
                 relay(zp, q % 2, q // 2).wait_send()
 
 
-def projected_part(R, C, orbitals, kernel, applied):
+def relayed(R, C, orbitals, kernel, applied, fit):
     Z = C // 2
     N, B = orbitals.shape
     NU, M = kernel.shape
+    G = fit.shape[1]
     at = applied.T
     J = at.shape[0]
+    NT = M // T
+    W = T // 2
     dma = pltpu.SemaphoreType.DMA
+    low, high = jnp.bfloat16, jnp.float32
+    tiles = pltpu.VMEM((NT, R * J, W), low)
     return pl.pallas_call(
-        functools.partial(gather_kernel, R, C),
-        out_shape=jax.ShapeDtypeStruct((R * J, M), jnp.float32),
-        in_specs=[pl.BlockSpec(memory_space=pl.ANY)] * 3,
+        functools.partial(whole_kernel, R, C),
+        out_shape=jax.ShapeDtypeStruct((J, G), low),
+        in_specs=[pl.BlockSpec(memory_space=pl.ANY)] * 4,
         out_specs=pl.BlockSpec(memory_space=pltpu.VMEM),
         scratch_shapes=[
-            pltpu.VMEM((Z, N, 2 * B), jnp.bfloat16),
-            pltpu.VMEM((Z, NU, 2 * B), jnp.bfloat16),
-            pltpu.VMEM((R * J, NU), jnp.bfloat16),
-            pltpu.VMEM((NU, M), jnp.bfloat16),
-            dma, dma,
+            pltpu.VMEM((Z, N, 2 * B), low),
+            pltpu.VMEM((Z, NU, 2 * B), low),
+            pltpu.VMEM((R * J, NU), low),
+            pltpu.VMEM((KS, NU, T), low),
+            pltpu.VMEM((M, G), low),
+            pltpu.VMEM((NT, R * J, W), high),
+            tiles, tiles, tiles, tiles, tiles, tiles,
+            pltpu.VMEM((NT, R * J, T), low),
+            pltpu.VMEM((R * J, G), high),
+            pltpu.VMEM((R - 1, J, G), low),
+            pltpu.VMEM((R - 1, J, G), low),
+            dma, dma((KS,)), dma,
             dma((Z, H)), dma((Z, H)), dma((Z, H)), dma((Z, H)),
             dma((Z, H)), dma((Z, H)), dma((Z, 2, H // 2)),
             dma((R,)), dma((R,)),
-        ],
+        ] + [dma((NT,))] * 8 + [dma((R - 1,))] * 2,
         compiler_params=pltpu.CompilerParams(
             collective_id=0, has_side_effects=True, vmem_limit_bytes=60 * 1024 * 1024),
-    )(orbitals, at, kernel)
+    )(orbitals, at, kernel, fit)
 
 
 def plain(orbitals, kernel, applied, fit):
@@ -291,18 +439,6 @@
     return result.astype(jnp.bfloat16)
 
 
-def relayed(R, C, orbitals, kernel, applied, fit):
-    partial_sum = projected_part(R, C, orbitals, kernel, applied)
-    projected = lax.psum(partial_sum, "col")
-    result = lax.psum_scatter(
-        -jnp.dot(projected.astype(jnp.bfloat16), fit, preferred_element_type=jnp.float32),
-        "row",
-        scatter_dimension=0,
-        tiled=True,
-    )
-    return result.astype(jnp.bfloat16)
-
-
 def solution(mesh):
     R, C = mesh.shape["row"], mesh.shape["col"]
 

time: 360 us -> 260 us (0.72)
  blocking collectives: 109 us -> 0 us
  Pallas kernels: 182 us -> 258 us
  waiting for transfers between devices: 43.4 us -> 0 us
  between operations: 13.4 us -> 0.01 us
  matrix products: 9.65 us -> 0 us
    psum x1 -> x0, blocking collectives: 109 us -> none  [relayed(): projected = lax.psum(partial_sum, 'col')]
    pallas_call x1, Pallas kernels: 182 us -> 258 us  [relayed(): pl.pallas_call(functools.partial(whole_kernel, R, C), out_shape=jax.Shape...]
    reduce_scatter x1 -> x0, waiting for transfers between devices: 43.3 us -> none  [relayed(): lax.psum_scatter(-jnp.dot(projected.astype(jnp.bfloat16), fit, preferred_...]
    dot_general x1 -> x0, matrix products: 9.65 us -> none  [relayed(): jnp.dot(projected.astype(jnp.bfloat16), fit, preferred_element_type=jnp.f...]
  transfers between devices with their start and end apart: 1 -> 0, of which waited for: 1 -> 0; matrix products, arithmetic and copies ran while one was open for 0% -> 0% of each run, Pallas kernels for 0% -> 0%
where the time goes in v2:
time: 260 us
  Pallas kernels  258 us (99%)
    pallas_call x1, Pallas kernels, relayed(): pl.pallas_call(functools.partial(whole_kernel, R, C), out_shape=jax.Shape...  258 us

profile of v2, /device:TPU:0, one launch (start us, length us, event | category | flops | bytes accessed | tf_op | source)
XLA Modules:
  0.0 259.6 jit_solution(562078086837384980)
XLA Ops:
  0.0 257.9 %shard_map.46 = bf16[64,2048]{1,0:T(8,128)(2,1)} custom-call(bf16[4096,128]{1,0:T(8,128)(2,1)} %orb.1, bf16[64,2048]{1,0:T(8,128)(2,1)} %bitcast.1, bf16[2048,4096]{1,0:T(8,128)(2,1)} %kern.1, bf16[4096,2048]{1,0:T(8,128)(2,1)} %fit.1), custom_call_target="tpu_custom_call" | custom-call | tf_op jit(solution)/shard_map/pallas_call | solution.py:386
  257.9 1.7 copy.6

commit v3 on v2

--- a/solution.py
+++ b/solution.py
@@ -108,7 +108,6 @@
     def relay(zp, kk, f):
         path = f % 2
         ref = cbuf.at[zp, crows(f), lanes(kk)]
-        last = (path == 0) == dx
         to = jnp.where(path == 0, jnp.where(dy, xn, yn), jnp.where(dx, yn, xn))
         return pltpu.make_async_remote_copy(
             ref, ref, pl_s.at[zp, 2 * f + kk], pl_r.at[zp, kk, f],
@@ -124,15 +123,12 @@
             device_id=((r + o) % R, c), device_id_type=MESH)
 
     def do_relay(zp, f):
-        @pl.when(jnp.logical_not(diag))
+        @pl.when(jnp.logical_not(diag) & relays(f))
         def _():
             for kk in range(2):
                 desc = relay(zp, kk, f)
                 desc.wait_recv()
-
-                @pl.when(relays(f))
-                def _():
-                    desc.start()
+                desc.start()
 
     def spread(zp, q, up, down):
         if up:
@@ -158,49 +154,49 @@
     acp = pltpu.make_async_copy(at, abuf.at[pl.ds(pl.multiple_of(r * J, J), J)], a_s.at[0])
     acp.start()
 
+    def relay_step(d, f):
+        if d == 0:
+            do_relay(z, f)
+            return
+
+        @pl.when(z - d >= 0)
+        def _():
+            do_relay(z - d, f)
+
+        @pl.when(z + d < Z)
+        def _():
+            do_relay(z + d, f)
+
+    for d in range(1, Z):
+        @pl.loop(0, H)
+        def _(q):
+            @pl.when(z - d >= 0)
+            def _():
+                line(z - d, q, True).wait_recv()
+                spread(z - d, q, True, False)
+
+            @pl.when(z + d < Z)
+            def _():
+                line(z + d, q, False).wait_recv()
+                spread(z + d, q, False, True)
+
+            @pl.when(q % 2 == 1)
+            def _():
+                relay_step(d - 1, q // 2)
+
     @pl.loop(0, HH)
     def _(f):
-        do_relay(z, f)
-
-    for d in range(1, Z):
-        below = z - d >= 0
-        above = z + d < Z
-
-        @pl.loop(0, H)
-        def _(q):
-            @pl.when(below)
-            def _():
-                line(z - d, q, True).wait_recv()
-                spread(z - d, q, True, False)
-
-            @pl.when(above)
-            def _():
-                line(z + d, q, False).wait_recv()
-                spread(z + d, q, False, True)
-
-            @pl.when((q % 2 == 1) & (q > 1))
-            def _():
-                @pl.when(below)
-                def _():
-                    do_relay(z - d, q // 2 - 1)
-
-                @pl.when(above)
-                def _():
-                    do_relay(z + d, q // 2 - 1)
-
-        @pl.when(below)
-        def _():
-            do_relay(z - d, HH - 1)
-
-        @pl.when(above)
-        def _():
-            do_relay(z + d, HH - 1)
+        relay_step(Z - 1, f)
 
     @pl.loop(0, Z)
     def _(zp):
         @pl.loop(0, H)
         def _(q):
             sibling(zp, q, 1 - k).wait_recv()
+
+            @pl.when(jnp.logical_not(diag) & jnp.logical_not(relays(q // 2)))
+            def _():
+                relay(zp, q % 2, q // 2).wait_recv()
 
     half = pl.ds(pl.multiple_of(k * (N // 2), N // 2), N // 2)
 

time: 260 us -> 176 us (0.68)
  Pallas kernels: 258 us -> 174 us
    pallas_call x1, Pallas kernels: 258 us -> 174 us  [relayed(): pl.pallas_call(functools.partial(whole_kernel, R, C), out_shape=jax.Shape...]
where the time goes in v3:
time: 176 us
  Pallas kernels  174 us (99%)
    pallas_call x1, Pallas kernels, relayed(): pl.pallas_call(functools.partial(whole_kernel, R, C), out_shape=jax.Shape...  174 us

profile of v3, /device:TPU:0, one launch (start us, length us, event | category | flops | bytes accessed | tf_op | source)
XLA Modules:
  0.0 175.7 jit_solution(3581382676965356994)
XLA Ops:
  0.0 174.0 %shard_map.46 = bf16[64,2048]{1,0:T(8,128)(2,1)} custom-call(bf16[4096,128]{1,0:T(8,128)(2,1)} %orb.1, bf16[64,2048]{1,0:T(8,128)(2,1)} %bitcast.1, bf16[2048,4096]{1,0:T(8,128)(2,1)} %kern.1, bf16[4096,2048]{1,0:T(8,128)(2,1)} %fit.1), custom_call_target="tpu_custom_call" | custom-call | tf_op jit(solution)/shard_map/pallas_call | solution.py:382
  174.0 1.7 copy.6
